TPU v7x, 512 devices: a whole 4x4x16 slice. The times are simulated.
512 devices in a mesh: replica: 32 (over z_lo, y, core), fsdp: 16 (over z_hi, x).
Axes of the slice: x: 4, y: 4, z: 16 (z_hi: 4, z_lo: 4; z = z_hi * 4 + z_lo), core: 2. Of those that a mesh axis runs over, the one named last changes fastest.
Arguments:
- activations: bfloat16 [32, 2048, 256], P('replica', 'fsdp'), may hold values from -6 to 6
- cotangent: bfloat16 [32, 2048, 4096], P('replica', 'fsdp'), may hold values from -0.125 to 0.125
- momentum: float32 [32, 256, 4096], P('replica', 'fsdp'), may hold values from -6 to 6
- kept_index: int32 [8], replicated, may hold values from 0 to 63, as said below
Outputs:
- update: bfloat16 [256, 4096], P('fsdp')
- momentum_out: float32 [32, 256, 4096], P('replica', 'fsdp')
Inputs may be any that keep to these rules, and one draw needn't show every extreme that they name: `kept_index`: 8 different numbers; 0 and 63 are always among them.
All inputs are finite; a program needn't handle non-finite values.
Results may differ from a plain program's by a relative error of at most 0.00085.
Values may be sent and summed in bfloat16 or wider, within the bound.
A program may use at most 192 MiB of HBM per device.

v0:
```python
import math

import jax
import jax.numpy as jnp
from jax import lax
from jax.sharding import PartitionSpec as P

decay_rate = 0.999


def group_basis(kept_index):
    sample_pos = jnp.arange(8, dtype=jnp.float32)
    frequency = jnp.arange(8, dtype=jnp.float32)
    weights = jnp.where(frequency == 0.0, math.sqrt(1.0 / 8.0), 0.5)
    cosine = (
        jnp.cos(math.pi * (2.0 * sample_pos[None, :] + 1.0) * frequency[:, None] / 16.0)
        * weights[:, None]
    )
    full_table = (cosine[:, None, :, None] * cosine[None, :, None, :]).reshape(64, 8, 8)
    selector = (kept_index[:, None] == jnp.arange(64, dtype=jnp.int32)[None, :]).astype(jnp.float32)
    return jnp.einsum("kc,cij->kij", selector, full_table, precision=lax.Precision.HIGHEST)


def encode_blocks(values_grid, basis_table):
    rows_all, width = values_grid.shape
    blocks = values_grid.reshape(rows_all // 8, 8, width // 8, 8)
    return jnp.einsum("kij,aibj->kab", basis_table, blocks, precision=lax.Precision.HIGHEST)


def decode_blocks(coeffs, basis_table):
    return jnp.einsum("kij,kab->aibj", basis_table, coeffs, precision=lax.Precision.HIGHEST)


def soft_sign(blocks):
    group_scale = jnp.sqrt(jnp.mean(blocks * blocks, axis=(1, 3), keepdims=True) + 1e-06)
    return jnp.tanh(blocks / group_scale)


def on_device(activations, cotangent, momentum, kept_index):
    local_inputs = activations[0]
    local_cotan = cotangent[0]
    local_moment = momentum[0]
    row_dev, width = local_moment.shape
    basis_table = group_basis(kept_index)
    gradient = lax.psum_scatter(
        lax.dot_general(
            local_inputs, local_cotan, (((0,), (0,)), ((), ())), preferred_element_type=jnp.float32
        ),
        "fsdp",
        scatter_dimension=0,
        tiled=True,
    )
    accrued = decay_rate * local_moment + gradient
    coeffs = encode_blocks(accrued, basis_table)
    momentum_out = accrued - decode_blocks(coeffs, basis_table).reshape(row_dev, width)
    total = lax.psum(coeffs, "replica")
    update = (
        soft_sign(decode_blocks(total, basis_table)).reshape(row_dev, width).astype(jnp.bfloat16)
    )
    return (update, momentum_out[None])


def solution(mesh):
    return jax.shard_map(
        on_device,
        mesh=mesh,
        in_specs=(
            P("replica", "fsdp", None),
            P("replica", "fsdp", None),
            P("replica", "fsdp", None),
            P(),
        ),
        out_specs=(P("fsdp", None), P("replica", "fsdp", None)),
        check_vma=False,
    )
```

profile of v0, /device:TPU:1, one launch (start us, length us, event | category | flops | bytes accessed | tf_op | source)
XLA Modules:
  0.0 335.5 jit_solution(2487045234596488563)
XLA Ops:
  7.2 0.0 copy-start
  7.2 0.0 copy-start.2
  7.2 0.0 copy-start.1
  7.2 0.0 reduce-scatter.2.cloned.1.call-start
  7.2 1.1 copy-done
  8.4 3.5 %fusion = f32[256,4096]{1,0:T(8,128)} fusion(bf16[1,128,4096]{2,1,0:T(8,128)(2,1)S(1)} %copy-done, bf16[1,128,256]{2,1,0:T(8,128)(2,1)} %param.4), kind=kOutput, calls=%fused_computation.2 | convolution fusion | flops 268435456 | bytes 5308416 | tf_op jit(solution)/shard_map/dot_general | solution.py:46
  11.9 0.0 reduce-scatter.2.cloned.1.call-update
  11.9 0.1 cosine_multiply_fusion
  12.0 0.1 mul.99
  12.1 0.1 mul.95
  12.2 0.1 mul.96
  12.3 0.0 copy-done.2
  12.3 0.3 convolution_bitcast_fusion.1
  12.6 160.8 %reduce-scatter.2.cloned.1.call-done = f32[16,4096]{1,0:T(8,128)} async-done(((f32[256,4096]{1,0:T(8,128)}), f32[16,4096]{1,0:T(8,128)}) %reduce-scatter.2.cloned.1.call-update) | async-done | bytes 262160 | tf_op jit(solution)/shard_map/reduce_scatter | solution.py:45
  173.4 0.0 copy-done.1
  173.4 1.0 bitcast_add_fusion
  174.4 3.6 %reshape.109 = f32[2,8,512,8]{3,2,1,0:T(8,128)} reshape(f32[16,4096]{1,0:T(8,128)S(1)} %bitcast_add_fusion) | data formatting | bytes 524288 | tf_op jit(solution)/shard_map/reshape | solution.py:26
  178.0 5.7 %fusion.12 = f32[8,2,512,1]{2,0,3,1:T(8,128)S(1)} fusion(f32[8,8,8,1]{2,0,1,3:T(8,128)S(1)} %convolution_bitcast_fusion.1, f32[2,8,512,8]{3,2,1,0:T(8,128)} %reshape.109), kind=kOutput, calls=%fused_computation.22 | convolution fusion | flops 6291456 | bytes 296960 | tf_op jit(solution)/shard_map/kij,aibj->kab/dot_general | solution.py:27
  183.7 1.1 convolution_bitcast_fusion
  184.8 130.6 %psum.7 = f32[8,2,512]{2,0,1:T(8,128)S(1)} all-reduce(f32[8,2,512]{2,0,1:T(8,128)S(1)} %bitcast.46), channel_id=1, replica_groups=mesh['replica'=32,'fsdp'=16] {'replica'}, use_global_device_ids=true, to_apply=%region_1.2 | all-reduce | flops 8192 | bytes 65536 | tf_op jit(solution)/shard_map/psum | solution.py:56
  315.4 0.4 multiply_reduce_fusion
  315.8 0.1 fusion.2
  315.9 1.0 copy.12
  316.9 3.6 %convert_element_type.12 = bf16[16,4096]{1,0:T(8,128)(2,1)} reshape(bf16[2,8,512,8]{3,2,1,0:T(8,128)(2,1)S(1)} %copy.12) | data formatting | bytes 262144 | tf_op jit(solution)/shard_map/convert_element_type | solution.py:58
  320.5 3.4 %copy.14 = f32[2,8,512,8]{3,2,1,0:T(8,128)} copy(f32[2,8,512,8]{2,3,1,0:T(8,128)} %convolution_bitcast_fusion) | data formatting | bytes 524288 | tf_op jit(solution)/shard_map/kij,kab->aibj/transpose | solution.py:31
  323.9 4.0 %reshape.110 = f32[16,4096]{1,0:T(8,128)S(1)} reshape(f32[2,8,512,8]{3,2,1,0:T(8,128)} %copy.14) | data formatting | bytes 524288 | tf_op jit(solution)/shard_map/reshape | solution.py:55
  327.9 0.7 subtract_bitcast_fusion
  (3 shorter events, 0.0 us)
Async XLA Ops:
  7.2 1.2 copy-start
  7.2 5.1 %copy-start.2 = (s32[8]{0:T(128)S(1)}, s32[8]{0:T(128)}, u32[]{:S(2)}) copy-start(s32[8]{0:T(128)} %param.7) | copy-start | bytes 100
  7.2 166.2 %copy-start.1 = (f32[1,16,4096]{2,1,0:T(8,128)S(1)}, f32[1,16,4096]{2,1,0:T(8,128)}, u32[]{:S(2)}) copy-start(f32[1,16,4096]{2,1,0:T(8,128)} %param.6) | copy-start | bytes 786436
  7.2 166.2 %reduce-scatter.2.cloned.1.call-start = ((), (), s32[]{:S(2)}) async-start(), calls=%async_computation.1 | async-start | bytes 4456448 | tf_op jit(solution)/shard_map/reduce_scatter | solution.py:45
Sparse Core Ops, SparseCore 0:
  12.2 161.1 reduce-scatter.1
where the time goes:
time: 340 us; the launch traced here: 336 us
  waiting for transfers between devices  161 us (47%)
  blocking collectives  131 us (39%)
  local copies, waits for them, and re-layouts  17 us (5%)
  between operations  14.1 us (4%)
  matrix products  11 us (3%)
    reduce_scatter x1, waiting for transfers between devices, on_device(): lax.psum_scatter(lax.dot_general(local_inputs, local_cotan, (((0,), (0,))...  161 us
    psum x1, blocking collectives, on_device(): total = lax.psum(coeffs, 'replica')  131 us
  transfers between devices with their start and end apart: 1, of which 1 were waited for; matrix products, arithmetic and copies ran while one was open for 0% of the time, Pallas kernels for 0%

commit v1 on v0

v1 whole, which is shorter than its diff:
```python
import functools
import math

import jax
import jax.numpy as jnp
import numpy as np
from jax import lax
from jax.experimental import pallas as pl
from jax.experimental.pallas import tpu as pltpu
from jax.sharding import PartitionSpec as P

MESH = pl.DeviceIdType.MESH
decay_rate = 0.999
f32, bf16 = jnp.float32, jnp.bfloat16
HIGHEST = lax.Precision.HIGHEST


def cosine_table():
    u, i = np.arange(8)[:, None], np.arange(128)[None, :] % 8
    weight = np.where(u == 0, math.sqrt(1.0 / 8.0), 0.5)
    return (weight * np.cos(math.pi * (2 * i + 1) * u / 16)).astype(np.float32)


def halves(value):
    high = value.astype(bf16)
    return high, (value - high.astype(f32)).astype(bf16)


def dot(a, b):
    return jnp.dot(a, b, preferred_element_type=f32)


def wait_bytes(ref, sem):
    pltpu.make_async_copy(ref, ref, sem).wait()


def kernel(kept, table, act, cot, mom, upd, mo, a_in, c_in, m_in, lhs, us, ur, q, qr, s2, s3, upd_v, mo_v,
           local_sem, out_sem, xs, xr, us_s, us_r, q_s, q_r, s2_s, s2_r, s3_s, s3_r):
    r, f = lax.axis_index("replica"), lax.axis_index("fsdp")
    zl, yc, h, x = r // 8, r % 8, f // 4, f % 4
    own_rows = pl.ds(pl.multiple_of(x * 128, 128), 128)
    local = [
        pltpu.make_async_copy(act, a_in.at[own_rows], local_sem.at[0]),
        pltpu.make_async_copy(cot.at[:, pl.ds(pl.multiple_of(x * 1024, 1024), 1024)], c_in.at[own_rows], local_sem.at[1]),
        pltpu.make_async_copy(mom, m_in, local_sem.at[2]),
    ]
    for copy in local:
        copy.start()

    barrier = pltpu.get_barrier_semaphore()

    def greet(who):
        pl.semaphore_signal(barrier, inc=1, device_id=who, device_id_type=MESH)

    fsdp_peer = lambda d: (r, (f + d) % 16)
    yc_peer = lambda d: (zl * 8 + (yc + d) % 8, f)
    z_peer = lambda d: (((zl + d) % 4) * 8 + yc, f)

    @pl.loop(1, 16)
    def _(d):
        greet(fsdp_peer(d))

    @pl.loop(1, 8)
    def _(d):
        greet(yc_peer(d))

    @pl.loop(1, 4)
    def _(d):
        greet(z_peer(d))

    pl.semaphore_wait(barrier, 25)

    def send(src, dst, ssem, rsem, who):
        pltpu.make_async_remote_copy(
            src_ref=src, dst_ref=dst, send_sem=ssem, recv_sem=rsem, device_id=who, device_id_type=MESH
        ).start()

    for d in (2, 1, 3):
        send(act, a_in.at[own_rows], xs.at[0], xr.at[0], (r, h * 4 + (x + d) % 4))
    for c in range(2):
        for d in (2, 1, 3):
            xt = (x + d) % 4
            columns = pl.ds(pl.multiple_of(xt * 1024 + 512 * c, 512), 512)
            send(cot.at[:, columns], c_in.at[own_rows, pl.ds(512 * c, 512)], xs.at[1 + c], xr.at[1 + c], (r, h * 4 + xt))

    k_at = lax.broadcasted_iota(jnp.int32, (8, 128), 0)
    number = jnp.zeros((8, 128), jnp.int32)
    for k in range(8):
        number = jnp.where(k_at == k, kept[k], number)
    row_freq, col_freq = number >> 3, number & 7
    cu = jnp.zeros((8, 128), f32)
    cv = jnp.zeros((8, 128), f32)
    for u in range(8):
        line = jnp.broadcast_to(table[u:u + 1, :], (8, 128))
        cu = jnp.where(row_freq == u, line, cu)
        cv = jnp.where(col_freq == u, line, cv)
    cv512 = jnp.concatenate([cv] * 4, axis=1)
    row_at = lax.broadcasted_iota(jnp.int32, (256, 256), 0)
    col_at = lax.broadcasted_iota(jnp.int32, (256, 256), 1)
    row_block = ((row_at >> 3) & 15) * 2 + (row_at >> 7)
    cu_tall = jnp.concatenate([jnp.concatenate([cu] * 2, axis=1)] * 32, axis=0)
    left = jnp.where((col_at >> 3) == row_block, cu_tall, 0.0)
    at0 = lax.broadcasted_iota(jnp.int32, (512, 128), 0) >> 3
    at1 = lax.broadcasted_iota(jnp.int32, (512, 128), 1)
    gather = [(at0 + 64 * p == at1).astype(bf16) for p in range(2)]
    to0 = lax.broadcasted_iota(jnp.int32, (128, 512), 0)
    to1 = lax.broadcasted_iota(jnp.int32, (128, 512), 1) >> 3
    spread = [(to1 + 64 * p == to0).astype(bf16) for p in range(2)]
    sq0 = lax.broadcasted_iota(jnp.int32, (128, 128), 0) >> 3
    sq1 = lax.broadcasted_iota(jnp.int32, (128, 128), 1) >> 3
    cu_square = jnp.where(sq0 == sq1, jnp.concatenate([cu] * 16, axis=0), 0.0)
    encode16, decode64 = cu_square[:16, :16], cu_square.T[:64, :64]

    def fold(even, odd):
        total = None
        for value, matrix in ((even, gather[0]), (odd, gather[1])):
            for part in halves(value):
                term = dot(part, matrix)
                total = term if total is None else total + term
        return total

    def decode(coeffs):
        out = []
        for p in range(2):
            wide = sum(dot(part, spread[p]) for part in halves(coeffs))
            wide = (wide.reshape(8, 8, 512) * cv512[None]).reshape(64, 512)
            out.append(jnp.dot(decode64, wide, precision=HIGHEST, preferred_element_type=f32))
        return out

    local[2].wait()
    mixed = jnp.dot(encode16, m_in[...], precision=HIGHEST, preferred_element_type=f32)
    mixed = (decay_rate * mixed).reshape(2, 8, 4096)
    strips = [
        jnp.concatenate([mixed[p, :, 512 * j:512 * (j + 1)] * cv512 for j in range(8)], axis=0) for p in range(2)
    ]
    mom_coeffs = fold(*strips)

    local[0].wait()
    wait_bytes(a_in.at[0:384], xr.at[0])
    act_t = a_in[...].astype(f32).T.astype(bf16)
    left_high = left.astype(bf16)
    left_rest = left - left_high.astype(f32)
    left_mid, left_low = halves(left_rest)
    mixed_act = dot(left_high, act_t) + dot(left_mid, act_t) + dot(left_low, act_t)
    high, low = halves(mixed_act)
    lhs[0:256] = act_t
    lhs[256:512] = high
    lhs[512:768] = low

    local[1].wait()
    for c in range(2):
        wait_bytes(c_in.at[0:384, 0:512], xr.at[1 + c])
        block = c_in[:, 512 * c:512 * (c + 1)]
        mix = dot(lhs[256:512], block) + dot(lhs[512:768], block)
        mix = (mix.reshape(32, 8, 512) * cv512[None]).reshape(256, 512)
        us[c, :, 0:8, :] = fold(mix[:128], mix[128:]).reshape(16, 8, 128)
        grad = dot(lhs[0:256], block).reshape(16, 2, 8, 512)
        size = jnp.maximum(jnp.abs(grad[:, 0]), jnp.abs(grad[:, 1]))
        size = functools.reduce(jnp.maximum, [size[:, :, 128 * g:128 * (g + 1)] for g in range(4)])
        size = jnp.maximum(size, 1e-33)
        us[c, :, 8:16, :] = size * (1.0 / 32767.0)

        @pl.loop(1, 16)
        def _(d):
            who = fsdp_peer(d)
            send(us.at[c, who[1]], ur.at[c, f], us_s.at[c], us_r.at[c], who)

        inverse = 32767.0 / size
        inverse = jnp.concatenate([inverse] * 4, axis=2)[:, None]
        q[c] = jnp.round(grad * inverse).astype(jnp.int32).astype(jnp.int16).reshape(16, 16, 512)

        @pl.loop(1, 16)
        def _(d):
            who = fsdp_peer(d)
            send(q.at[c, who[1]], qr.at[c, f], q_s.at[c], q_r.at[c], who)

        ur[c, pl.ds(f, 1)] = us[c, pl.ds(f, 1)]
        qr[c, pl.ds(f, 1)] = q[c, pl.ds(f, 1)]

    for c in range(2):
        wait_bytes(ur.at[c, 0:15], us_r.at[c])
    own = jnp.concatenate(
        [
            ur[c, xx, 0:8, :] + ur[c, 4 + xx, 0:8, :] + ur[c, 8 + xx, 0:8, :] + ur[c, 12 + xx, 0:8, :]
            for xx in range(4)
            for c in range(2)
        ],
        axis=0,
    )
    own = own + mom_coeffs

    s2[pl.ds(yc, 1)] = own[None]

    @pl.loop(1, 8)
    def _(d):
        send(s2.at[yc], s2.at[yc], s2_s, s2_r, yc_peer(d))

    removed = decode(own)
    wait_bytes(s2.at[0:7], s2_r)
    part = functools.reduce(jnp.add, [s2[i] for i in range(8)])
    s3[pl.ds(zl, 1)] = part[None]

    @pl.loop(1, 4)
    def _(d):
        send(s3.at[zl], s3.at[zl], s3_s, s3_r, z_peer(d))

    wait_bytes(s3.at[0:3], s3_r)
    total = s3[0] + s3[1] + s3[2] + s3[3]
    power = jnp.sum((total * total).reshape(8, 8, 128), axis=1, keepdims=True)
    scaled = (total.reshape(8, 8, 128) / jnp.sqrt(power * (1.0 / 64.0) + 1e-06)).reshape(64, 128)
    decoded = decode(scaled)
    for j in range(8):
        block = jnp.concatenate([decoded[p][8 * j:8 * j + 8] for p in range(2)], axis=0)
        upd_v[:, 512 * j:512 * (j + 1)] = jnp.tanh(block).astype(bf16)
    out0 = pltpu.make_async_copy(upd_v, upd, out_sem.at[0])
    out0.start()

    for c in range(2):
        wait_bytes(qr.at[c, 0:15], q_r.at[c])
    for xx in range(4):
        for c in range(2):
            j = 2 * xx + c
            columns = slice(512 * j, 512 * (j + 1))
            grad = None
            for hh in range(4):
                scale = jnp.concatenate([ur[c, 4 * hh + xx, 8:16, :]] * 4, axis=1)
                term = qr[c, 4 * hh + xx].astype(jnp.int32).astype(f32).reshape(2, 8, 512) * scale[None]
                grad = term if grad is None else grad + term
            for p in range(2):
                rows = slice(8 * p, 8 * p + 8)
                mo_v[rows, columns] = decay_rate * m_in[rows, columns] + grad[p] - removed[p][8 * j:8 * j + 8]
    out1 = pltpu.make_async_copy(mo_v, mo, out_sem.at[1])
    out1.start()

    wait_bytes(a_in.at[0:384], xs.at[0])
    for c in range(2):
        wait_bytes(c_in.at[0:384, 0:512], xs.at[1 + c])
        wait_bytes(us.at[c, 0:15], us_s.at[c])
        wait_bytes(q.at[c, 0:15], q_s.at[c])
    wait_bytes(s2.at[0:7], s2_s)
    wait_bytes(s3.at[0:3], s3_s)
    out0.wait()
    out1.wait()


def on_device(activations, cotangent, momentum, kept_index):
    hbm = pl.BlockSpec(memory_space=pl.ANY)
    dma = pltpu.SemaphoreType.DMA
    update, momentum_out = pl.pallas_call(
        kernel,
        name="outer_step",
        out_shape=(jax.ShapeDtypeStruct((16, 4096), bf16), jax.ShapeDtypeStruct((16, 4096), f32)),
        in_specs=[
            pl.BlockSpec(memory_space=pltpu.SMEM),
            pl.BlockSpec(memory_space=pltpu.VMEM),
            hbm,
            hbm,
            hbm,
        ],
        out_specs=(hbm, hbm),
        scratch_shapes=[
            pltpu.VMEM((512, 256), bf16),
            pltpu.VMEM((512, 1024), bf16),
            pltpu.VMEM((16, 4096), f32),
            pltpu.VMEM((768, 512), bf16),
            pltpu.VMEM((2, 16, 16, 128), f32),
            pltpu.VMEM((2, 16, 16, 128), f32),
            pltpu.VMEM((2, 16, 16, 512), jnp.int16),
            pltpu.VMEM((2, 16, 16, 512), jnp.int16),
            pltpu.VMEM((8, 64, 128), f32),
            pltpu.VMEM((4, 64, 128), f32),
            pltpu.VMEM((16, 4096), bf16),
            pltpu.VMEM((16, 4096), f32),
            dma((3,)),
            dma((2,)),
            dma((3,)),
            dma((3,)),
            dma((2,)),
            dma((2,)),
            dma((2,)),
            dma((2,)),
            dma,
            dma,
            dma,
            dma,
        ],
        compiler_params=pltpu.CompilerParams(
            collective_id=1, has_side_effects=True, vmem_limit_bytes=40 * 1024 * 1024
        ),
    )(kept_index, jnp.asarray(cosine_table()), activations[0], cotangent[0], momentum[0])
    return update, momentum_out[None]


def solution(mesh):
    return jax.shard_map(
        on_device,
        mesh=mesh,
        in_specs=(
            P("replica", "fsdp", None),
            P("replica", "fsdp", None),
            P("replica", "fsdp", None),
            P(),
        ),
        out_specs=(P("fsdp", None), P("replica", "fsdp", None)),
        check_vma=False,
    )
```

time: 340 us -> 78.3 us (0.23); the launches traced: 336 us -> 78.1 us
  waiting for transfers between devices: 161 us -> 0 us
  blocking collectives: 131 us -> 0 us
  Pallas kernels: 0 us -> 72.4 us
  between operations: 14.1 us -> 0.66 us
  local copies, waits for them, and re-layouts: 17 us -> 5.05 us
  matrix products: 11 us -> 0 us
    reduce_scatter x1 -> x0, waiting for transfers between devices: 161 us -> none  [on_device(): lax.psum_scatter(lax.dot_general(local_inputs, local_cotan, (((0,), (0,))...]
    psum x1 -> x0, blocking collectives: 131 us -> none  [on_device(): total = lax.psum(coeffs, 'replica')]
    pallas_call x0 -> x1, Pallas kernels: none -> 72.4 us  [on_device(): pl.pallas_call(kernel, name='outer_step', out_shape=(jax.ShapeDtypeStruct...]
    dot_general x5 -> x0, matrix products: 11 us -> none  [the longest x1 5.67 us: encode_blocks(): jnp.einsum('kij,aibj->kab', basis_table, blocks, precision=lax.Precision....]
    reshape x2 -> x0, local copies, waits for them, and re-layouts: 7.58 us -> none  [the longest x1 3.97 us: on_device(): decode_blocks(coeffs, basis_table).reshape(row_dev, width)]
    convert_element_type x2 -> x0, local copies, waits for them, and re-layouts: 4.59 us -> none  [on_device(): soft_sign(decode_blocks(total, basis_table)).reshape(row_dev, width)]
    unnamed x6 -> x12, local copies, waits for them, and re-layouts: 1.17 us -> 5.05 us
    transpose x1 -> x0, local copies, waits for them, and re-layouts: 3.44 us -> none  [decode_blocks(): jnp.einsum('kij,kab->aibj', basis_table, coeffs, precision=lax.Precision....]
  transfers between devices with their start and end apart: 1 -> 0, of which waited for: 1 -> 0; matrix products, arithmetic and copies ran while one was open for 0% -> 0% of each run, Pallas kernels for 0% -> 0%
where the time goes in v1:
time: 78.3 us; the launch traced here: 78.1 us
  Pallas kernels  72.4 us (92%)
  local copies, waits for them, and re-layouts  5.05 us (6%)
    pallas_call x1, Pallas kernels, on_device(): pl.pallas_call(kernel, name='outer_step', out_shape=(jax.ShapeDtypeStruct...  72.4 us
    unnamed x12, local copies, waits for them, and re-layouts  5.05 us

profile of v1, /device:TPU:1, one launch (start us, length us, event | category | flops | bytes accessed | tf_op | source)
XLA Modules:
  0.0 78.1 jit_solution(1374604479144920931)
XLA Ops:
  0.6 0.0 copy-start.3
  0.6 0.0 copy-start.4
  0.7 0.7 copy-done.3
  1.3 0.0 copy-done.4
  1.3 0.0 copy-start
  1.3 1.2 %copy-done = bf16[1,128,4096]{2,1,0:T(8,128)(2,1)S(1)} copy-done((bf16[1,128,4096]{2,1,0:T(8,128)(2,1)S(1)}, bf16[1,128,4096]{2,1,0:T(8,128)(2,1)}, u32[]{:S(2)}) %copy-start) | copy-done | bytes 1048600
  2.5 0.0 copy-start.1
  2.6 0.9 %copy-done.1 = f32[1,16,4096]{2,1,0:T(8,128)S(1)} copy-done((f32[1,16,4096]{2,1,0:T(8,128)S(1)}, f32[1,16,4096]{2,1,0:T(8,128)}, u32[]{:S(2)}) %copy-start.1) | copy-done | bytes 262168
  3.5 0.0 copy-start.2
  3.5 0.8 %copy-done.2 = bf16[1,128,256]{2,1,0:T(8,128)(2,1)S(1)} copy-done((bf16[1,128,256]{2,1,0:T(8,128)(2,1)S(1)}, bf16[1,128,256]{2,1,0:T(8,128)(2,1)}, u32[]{:S(2)}) %copy-start.2) | copy-done | bytes 65560
  4.3 72.4 %outer_step.1 = (bf16[16,4096]{1,0:T(8,128)(2,1)S(1)}, f32[16,4096]{1,0:T(8,128)S(1)}) custom-call(s32[8]{0:T(128)S(1)} %copy-done.4, f32[8,128]{1,0:T(8,128)S(1)} %copy-done.3, bf16[128,256]{1,0:T(8,128)(2,1)S(1)} %bitcast.7, bf16[128,4096]{1,0:T(8,128)(2,1)S(1)} %bitcast.4, f32[16,4096]{1,0:T(8,128)S(1)} %bitcast.5), custom_call_target="tpu_custom_call" | custom-call | tf_op jit(solution)/shard_map/outer_step/pallas_call | solution.py:249
  76.7 0.7 copy.9
  77.4 0.7 copy.10
Async XLA Ops:
  0.6 0.7 copy-start.3
  0.6 0.7 copy-start.4
  1.3 1.2 %copy-start = (bf16[1,128,4096]{2,1,0:T(8,128)(2,1)S(1)}, bf16[1,128,4096]{2,1,0:T(8,128)(2,1)}, u32[]{:S(2)}) copy-start(bf16[1,128,4096]{2,1,0:T(8,128)(2,1)} %param.6) | copy-start | bytes 3145732
  2.5 0.9 %copy-start.1 = (f32[1,16,4096]{2,1,0:T(8,128)S(1)}, f32[1,16,4096]{2,1,0:T(8,128)}, u32[]{:S(2)}) copy-start(f32[1,16,4096]{2,1,0:T(8,128)} %param.7) | copy-start | bytes 786436
  3.5 0.8 %copy-start.2 = (bf16[1,128,256]{2,1,0:T(8,128)(2,1)S(1)}, bf16[1,128,256]{2,1,0:T(8,128)(2,1)}, u32[]{:S(2)}) copy-start(bf16[1,128,256]{2,1,0:T(8,128)(2,1)} %param.5) | copy-start | bytes 196612

commit v2 on v0

v2 whole, which is shorter than its diff:
```python
import functools
import math

import jax
import jax.numpy as jnp
from jax import lax
from jax.experimental import pallas as pl
from jax.experimental.pallas import tpu as pltpu
from jax.sharding import PartitionSpec as P

MESH = pl.DeviceIdType.MESH
decay_rate = 0.999
f32, bf16 = jnp.float32, jnp.bfloat16
HIGHEST = lax.Precision.HIGHEST
WIDTHS = (384, 640)
STARTS = (0, 384)
CHUNKS = range(len(WIDTHS))


def halves(value):
    high = value.astype(bf16)
    return high, (value - high.astype(f32)).astype(bf16)


def dot(a, b):
    return jnp.dot(a, b, preferred_element_type=f32)


def exact(a, b):
    return jnp.dot(a, b, precision=HIGHEST, preferred_element_type=f32)


def iota(shape, dim):
    return lax.broadcasted_iota(jnp.int32, shape, dim)


def wait_bytes(ref, sem):
    pltpu.make_async_copy(ref, ref, sem).wait()


def cosine_table():
    u = iota((8, 128), 0)
    angle = ((2 * (iota((8, 128), 1) & 7) + 1) * u) & 31
    value = jnp.zeros((8, 128), f32)
    for m in range(32):
        value = jnp.where(angle == m, math.cos(math.pi * m / 16), value)
    return jnp.where(u == 0, math.sqrt(1.0 / 8.0), 0.5 * value)


def kernel(kept_hbm, act, cot, mom, upd, mo, kept, a_own, c_own, m_in, a_in, c_in, u1, u1r, u2, u2r, s3, s4,
           q0, q1, qr0, qr1, sc, scr, upd_v, mo_v, local_sem, out_sem, xs, xr, u1_s, u1_r, u2_s, u2_r, s3_s, s3_r,
           s4_s, s4_r, q_s, q_r, sc_s, sc_r, relay):
    q, qr = (q0, q1), (qr0, qr1)
    r, f = lax.axis_index("replica"), lax.axis_index("fsdp")
    zl, yc, h, x = r // 8, r % 8, f // 4, f % 4
    own_rows = pl.ds(pl.multiple_of(x * 128, 128), 128)
    local = [
        pltpu.make_async_copy(kept_hbm, kept, local_sem.at[0]),
        pltpu.make_async_copy(act, a_own, local_sem.at[1]),
        pltpu.make_async_copy(cot, c_own.at[0:128], local_sem.at[2]),
        pltpu.make_async_copy(cot, c_own.at[128:256], local_sem.at[3]),
        pltpu.make_async_copy(mom, m_in, local_sem.at[4]),
        pltpu.make_async_copy(act, a_in.at[own_rows], local_sem.at[5]),
        pltpu.make_async_copy(cot.at[:, pl.ds(pl.multiple_of(x * 1024, 1024), 1024)], c_in.at[own_rows], local_sem.at[6]),
    ]

    def signal(sem, who):
        pl.semaphore_signal(sem, inc=1, device_id=who, device_id_type=MESH)

    def send(src, dst, ssem, rsem, who):
        pltpu.make_async_remote_copy(
            src_ref=src, dst_ref=dst, send_sem=ssem, recv_sem=rsem, device_id=who, device_id_type=MESH
        ).start()

    def fsdp_peer(d):
        return (r, (f + d) % 16)

    def x_peer(d):
        return (r, h * 4 + (x + d) % 4)

    def h_peer(d):
        return (r, ((h + d) % 4) * 4 + x)

    def yc_peer(d):
        return (zl * 8 + (yc + d) % 8, f)

    def z_peer(d):
        return (((zl + d) % 4) * 8 + yc, f)

    barrier = pltpu.get_barrier_semaphore()
    for d in (1, 3):
        signal(barrier, h_peer(d))
    for d in (2, 1, 3):
        signal(barrier, z_peer(d))
        signal(barrier, x_peer(d))

    @pl.loop(1, 8)
    def _(d):
        signal(barrier, yc_peer(d))

    for copy in local:
        copy.start()

    table = cosine_table()
    local[0].wait()
    k_at = iota((8, 128), 0)
    number = jnp.zeros((8, 128), jnp.int32)
    for k in range(8):
        number = jnp.where(k_at == k, kept[k], number)
    row_freq, col_freq = number >> 3, number & 7
    cu = jnp.zeros((8, 128), f32)
    cv = jnp.zeros((8, 128), f32)
    for u in range(8):
        line = jnp.broadcast_to(table[u:u + 1, :], (8, 128))
        cu = jnp.where(row_freq == u, line, cu)
        cv = jnp.where(col_freq == u, line, cv)
    cv512 = jnp.concatenate([cv] * 4, axis=1)
    row_at = iota((256, 256), 0)
    row_block = ((row_at >> 3) & 15) * 2 + (row_at >> 7)
    cu_tall = jnp.concatenate([jnp.concatenate([cu] * 2, axis=1)] * 32, axis=0)
    left = jnp.where((iota((256, 256), 1) >> 3) == row_block, cu_tall, 0.0)
    gather = [((iota((512, 128), 0) >> 3) + 64 * p == iota((512, 128), 1)).astype(bf16) for p in range(2)]
    same = (iota((128, 128), 0) >> 3) == (iota((128, 128), 1) >> 3)
    block_sum = same.astype(bf16)
    cu_square = jnp.where(same, jnp.concatenate([cu] * 16, axis=0), 0.0)
    cu_turned = cu_square.T
    encode16, decode16, decode64 = cu_square[:16, :16], cu_turned[:16, :16], cu_turned[:64, :64]

    def fold(even, odd):
        total = None
        for value, matrix in ((even, gather[0]), (odd, gather[1])):
            for part in halves(value):
                term = dot(part, matrix)
                total = term if total is None else total + term
        return total

    pl.semaphore_wait(barrier, 15)
    for d in (1, 3):
        signal(relay.at[0], h_peer(d))
    for d in (1, 2, 3):
        signal(relay.at[0], x_peer(d))

    for d in (2, 1, 3):
        send(act, a_in.at[own_rows], xs.at[0], xr.at[0], x_peer(d))
    for c in CHUNKS:
        for d in (2, 1, 3):
            columns = pl.ds(pl.multiple_of(((x + d) % 4) * 1024 + STARTS[c], 128), WIDTHS[c])
            send(cot.at[:, columns], c_in.at[own_rows, pl.ds(STARTS[c], WIDTHS[c])], xs.at[1 + c], xr.at[1 + c], x_peer(d))

    left_high = left.astype(bf16)
    left_mid, left_low = halves(left - left_high.astype(f32))
    local[1].wait()
    own_t = a_own[...].astype(f32).T.astype(bf16)
    mixed_act = jnp.concatenate(halves(dot(left_high, own_t) + dot(left_mid, own_t) + dot(left_low, own_t)), axis=1)
    for at in (2, 3, 4):
        local[at].wait()

    @pl.loop(1, 9)
    def _(d):
        j = (yc + d) % 8
        columns = pl.ds(pl.multiple_of(j * 512, 512), 512)
        mix = dot(mixed_act, c_own[:, columns])
        mix = (mix.reshape(32, 8, 512) * cv512[None]).reshape(256, 512)
        u1[j] = fold(mix[:128], mix[128:])
        rows = exact(encode16, m_in[:, columns]) * decay_rate
        own = fold(rows[:8] * cv512, rows[8:] * cv512)
        at = pl.ds(pl.multiple_of(f * 8, 8), 8)
        u1[j, at, :] = u1[j, at, :] + own

        @pl.when(d < 8)
        def _():
            send(u1.at[j], u1r.at[yc], u1_s, u1_r, yc_peer(d))

    pl.semaphore_wait(relay.at[0], 5)
    for d in (1, 2, 3):
        signal(relay.at[1], x_peer(d))

    local[5].wait()
    wait_bytes(a_in.at[0:384], xr.at[0])
    act_t = a_in[...].astype(f32).T.astype(bf16)
    local[6].wait()

    def products(c):
        width, groups = WIDTHS[c], WIDTHS[c] // 128
        wait_bytes(c_in.at[0:384, pl.ds(STARTS[c], width)], xr.at[1 + c])
        grad = dot(act_t, c_in[:, STARTS[c]:STARTS[c] + width]).reshape(16, 16, width)
        size = jnp.abs(grad)
        size = functools.reduce(jnp.maximum, [size[:, :, 128 * g:128 * (g + 1)] for g in range(groups)])
        size = jnp.maximum(jnp.max(size, axis=1, keepdims=True), 1e-33)
        sc[c] = size * (1.0 / 32767.0)
        inverse = jnp.concatenate([32767.0 / size] * groups, axis=2)
        q[c][...] = jnp.round(grad * inverse).astype(jnp.int32).astype(jnp.int16)
        qr[c][pl.ds(f, 1)] = q[c][pl.ds(f, 1)]
        scr[c, pl.ds(f, 1)] = sc[c, pl.ds(f, 1)]

    def send_products(c):
        @pl.loop(1, 16)
        def _(d):
            who = fsdp_peer(d)
            send(sc.at[c, who[1]], scr.at[c, f], sc_s.at[c], sc_r.at[c], who)
            send(q[c].at[who[1]], qr[c].at[f], q_s.at[c], q_r.at[c], who)

    products(0)
    pl.semaphore_wait(relay.at[1], 3)
    send_products(0)

    u1r[pl.ds(yc, 1)] = u1[pl.ds(yc, 1)]
    wait_bytes(u1r.at[0:7], u1_r)
    u2[...] = functools.reduce(jnp.add, [u1r[i] for i in range(8)]).reshape(16, 8, 128)

    @pl.loop(1, 16)
    def _(d):
        who = fsdp_peer(d)
        send(u2.at[who[1]], u2r.at[f], u2_s, u2_r, who)

    u2r[pl.ds(f, 1)] = u2[pl.ds(f, 1)]

    products(1)
    send_products(1)

    wait_bytes(u2r.at[0:15], u2_r)
    s3[pl.ds(zl, 1)] = functools.reduce(jnp.add, [u2r[i] for i in range(16)])[None]
    for d in (2, 1, 3):
        send(s3.at[zl], s3.at[zl], s3_s, s3_r, z_peer(d))
    wait_bytes(s3.at[0:3], s3_r)
    s4[pl.ds(yc, 1)] = functools.reduce(jnp.add, [s3[i] for i in range(4)])[None]

    @pl.loop(1, 8)
    def _(d):
        send(s4.at[yc], s4.at[yc], s4_s, s4_r, yc_peer(d))

    def new_momentum(c):
        width, groups = WIDTHS[c], WIDTHS[c] // 128
        wait_bytes(scr.at[c, 0:15], sc_r.at[c])
        wait_bytes(qr[c].at[0:15], q_r.at[c])
        strips = []
        for xx in range(4):
            start = 1024 * xx + STARTS[c]
            accrued = decay_rate * m_in[:, start:start + width]
            for hh in range(4):
                scale = jnp.concatenate([scr[c, 4 * hh + xx]] * groups, axis=1)
                accrued = accrued + qr[c][4 * hh + xx].astype(jnp.int32).astype(f32) * scale
            strips.append(accrued)
        accrued = jnp.concatenate(strips, axis=1)
        weight = jnp.concatenate([jnp.concatenate([cv] * 2, axis=0)] * (4 * groups), axis=1)
        rows = exact(encode16, accrued) * weight
        tall = jnp.concatenate([rows[:, 128 * g:128 * (g + 1)] for g in range(4 * groups)], axis=0)
        tall = functools.reduce(jnp.add, [dot(part, block_sum) for part in halves(tall)])
        rows = jnp.concatenate([tall[16 * g:16 * (g + 1)] for g in range(4 * groups)], axis=1)
        left_over = accrued - exact(decode16, rows * weight)
        for xx in range(4):
            start = 1024 * xx + STARTS[c]
            mo_v[:, start:start + width] = left_over[:, xx * width:(xx + 1) * width]

    new_momentum(0)

    wait_bytes(s4.at[0:7], s4_r)
    total = s4[...]
    power = jnp.sum(total * total, axis=1, keepdims=True)
    scaled = halves((total / jnp.sqrt(power * (1.0 / 64.0) + 1e-06)).reshape(64, 128))
    for p in range(2):
        spread = ((iota((128, 512), 1) >> 3) + 64 * p == iota((128, 512), 0)).astype(bf16)
        wide = dot(scaled[0], spread) + dot(scaled[1], spread)
        wide = (wide.reshape(8, 8, 512) * cv512[None]).reshape(64, 512)
        wide = jnp.tanh(exact(decode64, wide))
        for j in range(8):
            mo_half = wide[8 * j:8 * j + 8]
            upd_v[8 * p:8 * p + 8, 512 * j:512 * (j + 1)] = mo_half.astype(bf16)
    out0 = pltpu.make_async_copy(upd_v, upd, out_sem.at[0])
    out0.start()

    new_momentum(1)
    out1 = pltpu.make_async_copy(mo_v, mo, out_sem.at[1])
    out1.start()

    wait_bytes(a_in.at[0:384], xs.at[0])
    for c in CHUNKS:
        wait_bytes(c_in.at[0:384, pl.ds(STARTS[c], WIDTHS[c])], xs.at[1 + c])
        wait_bytes(sc.at[c, 0:15], sc_s.at[c])
        wait_bytes(q[c].at[0:15], q_s.at[c])
    wait_bytes(u1.at[0:7], u1_s)
    wait_bytes(u2.at[0:15], u2_s)
    wait_bytes(s3.at[0:3], s3_s)
    wait_bytes(s4.at[0:7], s4_s)
    out0.wait()
    out1.wait()


def on_device(activations, cotangent, momentum, kept_index):
    hbm = pl.BlockSpec(memory_space=pl.ANY)
    dma = pltpu.SemaphoreType.DMA
    vmem = pltpu.VMEM
    n = len(WIDTHS)
    update, momentum_out = pl.pallas_call(
        kernel,
        name="outer_step",
        out_shape=(jax.ShapeDtypeStruct((16, 4096), bf16), jax.ShapeDtypeStruct((16, 4096), f32)),
        in_specs=[hbm] * 4,
        out_specs=(hbm, hbm),
        scratch_shapes=[
            pltpu.SMEM((8,), jnp.int32),
            vmem((128, 256), bf16),
            vmem((256, 4096), bf16),
            vmem((16, 4096), f32),
            vmem((512, 256), bf16),
            vmem((512, 1024), bf16),
            vmem((8, 128, 128), f32),
            vmem((8, 128, 128), f32),
            vmem((16, 8, 128), f32),
            vmem((16, 8, 128), f32),
            vmem((4, 8, 128), f32),
            vmem((8, 8, 128), f32),
            *[vmem((16, 16, w), jnp.int16) for w in WIDTHS],
            *[vmem((16, 16, w), jnp.int16) for w in WIDTHS],
            vmem((n, 16, 1, 128), f32),
            vmem((n, 16, 1, 128), f32),
            vmem((16, 4096), bf16),
            vmem((16, 4096), f32),
            dma((7,)),
            dma((2,)),
            dma((1 + n,)),
            dma((1 + n,)),
            *[dma] * 8,
            dma((n,)),
            dma((n,)),
            dma((n,)),
            dma((n,)),
            pltpu.SemaphoreType.REGULAR((2,)),
        ],
        compiler_params=pltpu.CompilerParams(
            collective_id=1, has_side_effects=True, vmem_limit_bytes=60 * 1024 * 1024
        ),
    )(kept_index, activations[0], cotangent[0], momentum[0])
    return update, momentum_out[None]


def solution(mesh):
    return jax.shard_map(
        on_device,
        mesh=mesh,
        in_specs=(
            P("replica", "fsdp", None),
            P("replica", "fsdp", None),
            P("replica", "fsdp", None),
            P(),
        ),
        out_specs=(P("fsdp", None), P("replica", "fsdp", None)),
        check_vma=False,
    )
```

time: 340 us -> 61.7 us (0.18); the launches traced: 336 us -> 61.6 us
  waiting for transfers between devices: 161 us -> 0 us
  blocking collectives: 131 us -> 0 us
  Pallas kernels: 0 us -> 58.6 us
  local copies, waits for them, and re-layouts: 17 us -> 2.32 us
  between operations: 14.1 us -> 0.65 us
  matrix products: 11 us -> 0 us
    reduce_scatter x1 -> x0, waiting for transfers between devices: 161 us -> none  [on_device(): lax.psum_scatter(lax.dot_general(local_inputs, local_cotan, (((0,), (0,))...]
    psum x1 -> x0, blocking collectives: 131 us -> none  [on_device(): total = lax.psum(coeffs, 'replica')]
    pallas_call x0 -> x1, Pallas kernels: none -> 58.6 us  [on_device(): pl.pallas_call(kernel, name='outer_step', out_shape=(jax.ShapeDtypeStruct...]
    dot_general x5 -> x0, matrix products: 11 us -> none  [the longest x1 5.67 us: encode_blocks(): jnp.einsum('kij,aibj->kab', basis_table, blocks, precision=lax.Precision....]
    reshape x2 -> x0, local copies, waits for them, and re-layouts: 7.58 us -> none  [the longest x1 3.97 us: on_device(): decode_blocks(coeffs, basis_table).reshape(row_dev, width)]
    convert_element_type x2 -> x0, local copies, waits for them, and re-layouts: 4.59 us -> none  [on_device(): soft_sign(decode_blocks(total, basis_table)).reshape(row_dev, width)]
    transpose x1 -> x0, local copies, waits for them, and re-layouts: 3.44 us -> none  [decode_blocks(): jnp.einsum('kij,kab->aibj', basis_table, coeffs, precision=lax.Precision....]
  transfers between devices with their start and end apart: 1 -> 0, of which waited for: 1 -> 0; matrix products, arithmetic and copies ran while one was open for 0% -> 0% of each run, Pallas kernels for 0% -> 0%
where the time goes in v2:
time: 61.7 us; the launch traced here: 61.6 us
  Pallas kernels  58.6 us (95%)
  local copies, waits for them, and re-layouts  2.32 us (4%)
  between operations  0.65 us (1%)
    pallas_call x1, Pallas kernels, on_device(): pl.pallas_call(kernel, name='outer_step', out_shape=(jax.ShapeDtypeStruct...  58.6 us
    unnamed x4, local copies, waits for them, and re-layouts  2.32 us

profile of v2, /device:TPU:1, one launch (start us, length us, event | category | flops | bytes accessed | tf_op | source)
XLA Modules:
  0.0 61.6 jit_solution(16953154593761141262)
XLA Ops:
  0.6 58.6 %outer_step.1 = (bf16[16,4096]{1,0:T(8,128)(2,1)}, f32[16,4096]{1,0:T(8,128)}) custom-call(s32[8]{0:T(128)} %kept_hbm.1, bf16[128,256]{1,0:T(8,128)(2,1)} %bitcast.7, bf16[128,4096]{1,0:T(8,128)(2,1)} %bitcast.4, f32[16,4096]{1,0:T(8,128)} %bitcast.5), custom_call_target="tpu_custom_call" | custom-call | tf_op jit(solution)/shard_map/outer_step/pallas_call | solution.py:294
  59.2 0.0 copy-start
  59.3 1.6 %copy.8 = bf16[16,4096]{1,0:T(8,128)(2,1)} copy(bf16[16,4096]{1,0:T(8,128)(2,1)} %get-tuple-element.8) | data formatting | bytes 262144
  60.9 0.0 copy-done
  60.9 0.7 %copy.9 = f32[1,16,4096]{2,1,0:T(8,128)} copy(f32[1,16,4096]{2,1,0:T(8,128)S(1)} %bitcast.6) | data formatting | bytes 524288
Async XLA Ops:
  59.2 1.6 %copy-start = (f32[16,4096]{1,0:T(8,128)S(1)}, f32[16,4096]{1,0:T(8,128)}, u32[]{:S(2)}) copy-start(f32[16,4096]{1,0:T(8,128)} %get-tuple-element.5) | copy-start | bytes 786436

commit v3 on v2

--- a/solution.py
+++ b/solution.py
@@ -11,9 +11,8 @@
 MESH = pl.DeviceIdType.MESH
 decay_rate = 0.999
 f32, bf16 = jnp.float32, jnp.bfloat16
-HIGHEST = lax.Precision.HIGHEST
-WIDTHS = (384, 640)
-STARTS = (0, 384)
+WIDTHS = (256, 256, 256, 256)
+STARTS = tuple(sum(WIDTHS[:c]) for c in range(len(WIDTHS)))
 CHUNKS = range(len(WIDTHS))
 
 
@@ -26,8 +25,9 @@
     return jnp.dot(a, b, preferred_element_type=f32)
 
 
-def exact(a, b):
-    return jnp.dot(a, b, precision=HIGHEST, preferred_element_type=f32)
+def mix_rows(columns, value):
+    wide = [jnp.concatenate([c] * (value.shape[-1] // 128), axis=1) for c in columns]
+    return functools.reduce(jnp.add, [w * value[..., i:i + 1, :] for i, w in enumerate(wide)])
 
 
 def iota(shape, dim):
@@ -48,9 +48,8 @@
 
 
 def kernel(kept_hbm, act, cot, mom, upd, mo, kept, a_own, c_own, m_in, a_in, c_in, u1, u1r, u2, u2r, s3, s4,
-           q0, q1, qr0, qr1, sc, scr, upd_v, mo_v, local_sem, out_sem, xs, xr, u1_s, u1_r, u2_s, u2_r, s3_s, s3_r,
-           s4_s, s4_r, q_s, q_r, sc_s, sc_r, relay):
-    q, qr = (q0, q1), (qr0, qr1)
+           g, q, qr, qh, sc, scr, sch, upd_v, mo_v, local_sem, out_sem, xs, xr, u1_s, u1_r, u2_s, u2_r, s3_s, s3_r,
+           s4_s, s4_r, q_s, q_r, qh_s, qh_r, sc_s, sc_r, sch_s, sch_r, relay):
     r, f = lax.axis_index("replica"), lax.axis_index("fsdp")
     zl, yc, h, x = r // 8, r % 8, f // 4, f % 4
     own_rows = pl.ds(pl.multiple_of(x * 128, 128), 128)
@@ -119,20 +118,16 @@
     row_block = ((row_at >> 3) & 15) * 2 + (row_at >> 7)
     cu_tall = jnp.concatenate([jnp.concatenate([cu] * 2, axis=1)] * 32, axis=0)
     left = jnp.where((iota((256, 256), 1) >> 3) == row_block, cu_tall, 0.0)
-    gather = [((iota((512, 128), 0) >> 3) + 64 * p == iota((512, 128), 1)).astype(bf16) for p in range(2)]
-    same = (iota((128, 128), 0) >> 3) == (iota((128, 128), 1) >> 3)
-    block_sum = same.astype(bf16)
-    cu_square = jnp.where(same, jnp.concatenate([cu] * 16, axis=0), 0.0)
-    cu_turned = cu_square.T
-    encode16, decode16, decode64 = cu_square[:16, :16], cu_turned[:16, :16], cu_turned[:64, :64]
-
-    def fold(even, odd):
-        total = None
-        for value, matrix in ((even, gather[0]), (odd, gather[1])):
-            for part in halves(value):
-                term = dot(part, matrix)
-                total = term if total is None else total + term
-        return total
+    gather = ((iota((512, 128), 0) >> 3) == iota((512, 128), 1)).astype(bf16)
+    block_sum = ((iota((128, 128), 0) >> 3) == (iota((128, 128), 1) >> 3)).astype(bf16)
+    encode_rows = [jnp.broadcast_to(cu[:, i:i + 1], (8, 128)) for i in range(8)]
+    cu_turned = jnp.concatenate([cu] * 16, axis=0).T[:8, :8]
+    decode_rows = [jnp.broadcast_to(cu_turned[:, k:k + 1], (8, 128)) for k in range(8)]
+
+    def two_part(value, matrix):
+        n = value.shape[0]
+        both = dot(jnp.concatenate(halves(value), axis=0), matrix)
+        return both[:n] + both[n:]
 
     pl.semaphore_wait(barrier, 15)
     for d in (1, 3):
@@ -160,12 +155,12 @@
         j = (yc + d) % 8
         columns = pl.ds(pl.multiple_of(j * 512, 512), 512)
         mix = dot(mixed_act, c_own[:, columns])
-        mix = (mix.reshape(32, 8, 512) * cv512[None]).reshape(256, 512)
-        u1[j] = fold(mix[:128], mix[128:])
-        rows = exact(encode16, m_in[:, columns]) * decay_rate
-        own = fold(rows[:8] * cv512, rows[8:] * cv512)
+        rows = mix_rows(encode_rows, (m_in[:, columns] * decay_rate).reshape(2, 8, 512))
+        mix = (jnp.concatenate([mix.reshape(32, 8, 512), rows], axis=0) * cv512[None]).reshape(272, 512)
+        sums = two_part(mix, gather)
+        u1[j] = sums[:128] + pltpu.roll(sums[128:256], 64, 1)
         at = pl.ds(pl.multiple_of(f * 8, 8), 8)
-        u1[j, at, :] = u1[j, at, :] + own
+        u1[j, at, :] = u1[j, at, :] + sums[256:264] + pltpu.roll(sums[264:272], 64, 1)
 
         @pl.when(d < 8)
         def _():
@@ -180,29 +175,56 @@
     act_t = a_in[...].astype(f32).T.astype(bf16)
     local[6].wait()
 
+    up, down, across = (h + 1) % 4, (h + 3) % 4, (h + 2) % 4
+
+    def quantize(c, at, grad):
+        groups = WIDTHS[c] // 128
+        size = jnp.abs(grad)
+        size = functools.reduce(jnp.maximum, [size[:, :, 128 * i:128 * (i + 1)] for i in range(groups)])
+        size = jnp.maximum(jnp.max(size, axis=1, keepdims=True), 1e-33)
+        sc[c, at] = size * (1.0 / 32767.0)
+        inverse = jnp.concatenate([32767.0 / size] * groups, axis=2)
+        q[c][at] = jnp.round(grad * inverse).astype(jnp.int32).astype(jnp.int16)
+
+    def restore(c, value, scale):
+        return value.astype(jnp.int32).astype(f32) * jnp.concatenate([scale] * (WIDTHS[c] // 128), axis=-1)
+
+    def send_block(c, hh, xx, slot):
+        at, who = hh * 4 + xx, (r, hh * 4 + xx)
+        send(sc.at[c, at], scr.at[c, slot], sc_s.at[c], sc_r.at[c], who)
+        send(q[c].at[at], qr[c].at[slot], q_s.at[c], q_r.at[c], who)
+
     def products(c):
-        width, groups = WIDTHS[c], WIDTHS[c] // 128
-        wait_bytes(c_in.at[0:384, pl.ds(STARTS[c], width)], xr.at[1 + c])
-        grad = dot(act_t, c_in[:, STARTS[c]:STARTS[c] + width]).reshape(16, 16, width)
-        size = jnp.abs(grad)
-        size = functools.reduce(jnp.maximum, [size[:, :, 128 * g:128 * (g + 1)] for g in range(groups)])
-        size = jnp.maximum(jnp.max(size, axis=1, keepdims=True), 1e-33)
-        sc[c] = size * (1.0 / 32767.0)
-        inverse = jnp.concatenate([32767.0 / size] * groups, axis=2)
-        q[c][...] = jnp.round(grad * inverse).astype(jnp.int32).astype(jnp.int16)
-        qr[c][pl.ds(f, 1)] = q[c][pl.ds(f, 1)]
-        scr[c, pl.ds(f, 1)] = sc[c, pl.ds(f, 1)]
-
-    def send_products(c):
-        @pl.loop(1, 16)
-        def _(d):
-            who = fsdp_peer(d)
-            send(sc.at[c, who[1]], scr.at[c, f], sc_s.at[c], sc_r.at[c], who)
-            send(q[c].at[who[1]], qr[c].at[f], q_s.at[c], q_r.at[c], who)
+        wait_bytes(c_in.at[0:384, pl.ds(STARTS[c], WIDTHS[c])], xr.at[1 + c])
+        grad = dot(act_t, c_in[:, STARTS[c]:STARTS[c] + WIDTHS[c]]).reshape(16, 16, WIDTHS[c])
+        g[c][...] = grad
+        quantize(c, slice(None), grad)
+        for side, hh in ((0, up), (1, down)):
+            at, who = pl.ds(across * 4 + 2 * side, 2), (r, hh * 4 + x)
+            send(sc.at[c, at], sch.at[c, side], sch_s.at[c, side], sch_r.at[c, side], who)
+            send(q[c].at[at], qh[c].at[side], qh_s.at[c, side], qh_r.at[c, side], who)
+
+    def send_plain(c):
+        for xx in (2, 3):
+            send_block(c, up, xx, x)
+            send_block(c, down, xx - 2, 4 + x)
+        for d in (2, 1, 3):
+            send_block(c, h, (x + d) % 4, 8 + x)
+        qr[c][pl.ds(8 + x, 1)] = q[c][pl.ds(f, 1)]
+        scr[c, pl.ds(8 + x, 1)] = sc[c, pl.ds(f, 1)]
+
+    def send_sums(c):
+        for side, hh in ((0, up), (1, down)):
+            at = pl.ds(hh * 4 + 2 * side, 2)
+            wait_bytes(sch.at[c, side], sch_r.at[c, side])
+            wait_bytes(qh[c].at[side], qh_r.at[c, side])
+            quantize(c, at, g[c][at] + restore(c, qh[c][side], sch[c, side]))
+            for xx in (0, 1):
+                send_block(c, hh, xx + 2 * side, 4 * side + x)
 
     products(0)
     pl.semaphore_wait(relay.at[1], 3)
-    send_products(0)
+    send_plain(0)
 
     u1r[pl.ds(yc, 1)] = u1[pl.ds(yc, 1)]
     wait_bytes(u1r.at[0:7], u1_r)
@@ -216,12 +238,20 @@
     u2r[pl.ds(f, 1)] = u2[pl.ds(f, 1)]
 
     products(1)
-    send_products(1)
+    send_plain(1)
+    products(2)
+    send_plain(2)
+    send_sums(0)
+    products(3)
+    send_plain(3)
+    send_sums(1)
+    send_sums(2)
 
     wait_bytes(u2r.at[0:15], u2_r)
     s3[pl.ds(zl, 1)] = functools.reduce(jnp.add, [u2r[i] for i in range(16)])[None]
     for d in (2, 1, 3):
         send(s3.at[zl], s3.at[zl], s3_s, s3_r, z_peer(d))
+    send_sums(3)
     wait_bytes(s3.at[0:3], s3_r)
     s4[pl.ds(yc, 1)] = functools.reduce(jnp.add, [s3[i] for i in range(4)])[None]
 
@@ -231,53 +261,56 @@
 
     def new_momentum(c):
         width, groups = WIDTHS[c], WIDTHS[c] // 128
-        wait_bytes(scr.at[c, 0:15], sc_r.at[c])
-        wait_bytes(qr[c].at[0:15], q_r.at[c])
+        wait_bytes(scr.at[c, 0:11], sc_r.at[c])
+        wait_bytes(qr[c].at[0:11], q_r.at[c])
         strips = []
         for xx in range(4):
             start = 1024 * xx + STARTS[c]
             accrued = decay_rate * m_in[:, start:start + width]
-            for hh in range(4):
-                scale = jnp.concatenate([scr[c, 4 * hh + xx]] * groups, axis=1)
-                accrued = accrued + qr[c][4 * hh + xx].astype(jnp.int32).astype(f32) * scale
+            for slot in (xx, 4 + xx, 8 + xx):
+                accrued = accrued + restore(c, qr[c][slot], scr[c, slot])
             strips.append(accrued)
         accrued = jnp.concatenate(strips, axis=1)
-        weight = jnp.concatenate([jnp.concatenate([cv] * 2, axis=0)] * (4 * groups), axis=1)
-        rows = exact(encode16, accrued) * weight
+        weight = jnp.concatenate([cv] * (4 * groups), axis=1)[None]
+        rows = (mix_rows(encode_rows, accrued.reshape(2, 8, 4 * width)) * weight).reshape(16, 4 * width)
         tall = jnp.concatenate([rows[:, 128 * g:128 * (g + 1)] for g in range(4 * groups)], axis=0)
-        tall = functools.reduce(jnp.add, [dot(part, block_sum) for part in halves(tall)])
+        tall = two_part(tall, block_sum)
         rows = jnp.concatenate([tall[16 * g:16 * (g + 1)] for g in range(4 * groups)], axis=1)
-        left_over = accrued - exact(decode16, rows * weight)
+        rows = rows.reshape(2, 8, 4 * width) * weight
+        left_over = accrued - mix_rows(decode_rows, rows).reshape(16, 4 * width)
         for xx in range(4):
             start = 1024 * xx + STARTS[c]
             mo_v[:, start:start + width] = left_over[:, xx * width:(xx + 1) * width]
 
-    new_momentum(0)
+    for c in CHUNKS[:-1]:
+        new_momentum(c)
 
     wait_bytes(s4.at[0:7], s4_r)
     total = s4[...]
     power = jnp.sum(total * total, axis=1, keepdims=True)
-    scaled = halves((total / jnp.sqrt(power * (1.0 / 64.0) + 1e-06)).reshape(64, 128))
+    scaled = (total / jnp.sqrt(power * (1.0 / 64.0) + 1e-06)).reshape(64, 128)
+    bands = []
     for p in range(2):
         spread = ((iota((128, 512), 1) >> 3) + 64 * p == iota((128, 512), 0)).astype(bf16)
-        wide = dot(scaled[0], spread) + dot(scaled[1], spread)
-        wide = (wide.reshape(8, 8, 512) * cv512[None]).reshape(64, 512)
-        wide = jnp.tanh(exact(decode64, wide))
-        for j in range(8):
-            mo_half = wide[8 * j:8 * j + 8]
-            upd_v[8 * p:8 * p + 8, 512 * j:512 * (j + 1)] = mo_half.astype(bf16)
+        wide = two_part(scaled, spread).reshape(8, 8, 512) * cv512[None]
+        bands.append(jnp.tanh(mix_rows(decode_rows, wide)))
+    for j in range(8):
+        upd_v[:, 512 * j:512 * (j + 1)] = jnp.concatenate([band[j] for band in bands], axis=0).astype(bf16)
     out0 = pltpu.make_async_copy(upd_v, upd, out_sem.at[0])
     out0.start()
 
-    new_momentum(1)
+    new_momentum(CHUNKS[-1])
     out1 = pltpu.make_async_copy(mo_v, mo, out_sem.at[1])
     out1.start()
 
     wait_bytes(a_in.at[0:384], xs.at[0])
     for c in CHUNKS:
         wait_bytes(c_in.at[0:384, pl.ds(STARTS[c], WIDTHS[c])], xs.at[1 + c])
-        wait_bytes(sc.at[c, 0:15], sc_s.at[c])
-        wait_bytes(q[c].at[0:15], q_s.at[c])
+        wait_bytes(sc.at[c, 0:11], sc_s.at[c])
+        wait_bytes(q[c].at[0:11], q_s.at[c])
+        for side in range(2):
+            wait_bytes(sch.at[c, side], sch_s.at[c, side])
+            wait_bytes(qh[c].at[side], qh_s.at[c, side])
     wait_bytes(u1.at[0:7], u1_s)
     wait_bytes(u2.at[0:15], u2_s)
     wait_bytes(s3.at[0:3], s3_s)
@@ -310,10 +343,13 @@
             vmem((16, 8, 128), f32),
             vmem((4, 8, 128), f32),
             vmem((8, 8, 128), f32),
-            *[vmem((16, 16, w), jnp.int16) for w in WIDTHS],
-            *[vmem((16, 16, w), jnp.int16) for w in WIDTHS],
+            [vmem((16, 16, w), f32) for w in WIDTHS],
+            [vmem((16, 16, w), jnp.int16) for w in WIDTHS],
+            [vmem((12, 16, w), jnp.int16) for w in WIDTHS],
+            [vmem((2, 2, 16, w), jnp.int16) for w in WIDTHS],
             vmem((n, 16, 1, 128), f32),
-            vmem((n, 16, 1, 128), f32),
+            vmem((n, 12, 1, 128), f32),
+            vmem((n, 2, 2, 1, 128), f32),
             vmem((16, 4096), bf16),
             vmem((16, 4096), f32),
             dma((7,)),
@@ -323,8 +359,12 @@
             *[dma] * 8,
             dma((n,)),
             dma((n,)),
+            dma((n, 2)),
+            dma((n, 2)),
             dma((n,)),
             dma((n,)),
+            dma((n, 2)),
+            dma((n, 2)),
             pltpu.SemaphoreType.REGULAR((2,)),
         ],
         compiler_params=pltpu.CompilerParams(

time: 61.7 us -> 56.4 us (0.914)
  the two profiles are of different devices: /device:TPU:1 before, /device:TPU:3 now
where the time goes in v3:
time: 56.4 us; the launch traced here: 56.2 us
  Pallas kernels  53.2 us (94%)
  local copies, waits for them, and re-layouts  2.32 us (4%)
  between operations  0.65 us (1%)
    pallas_call x1, Pallas kernels, on_device(): pl.pallas_call(kernel, name='outer_step', out_shape=(jax.ShapeDtypeStruct...  53.2 us
    unnamed x4, local copies, waits for them, and re-layouts  2.32 us

profile of v3, /device:TPU:3, one launch (start us, length us, event | category | flops | bytes accessed | tf_op | source)
XLA Modules:
  0.0 56.2 jit_solution(2751652986432476969)
XLA Ops:
  0.6 53.2 %outer_step.1 = (bf16[16,4096]{1,0:T(8,128)(2,1)}, f32[16,4096]{1,0:T(8,128)}) custom-call(s32[8]{0:T(128)} %kept_hbm.1, bf16[128,256]{1,0:T(8,128)(2,1)} %bitcast.7, bf16[128,4096]{1,0:T(8,128)(2,1)} %bitcast.4, f32[16,4096]{1,0:T(8,128)} %bitcast.5), custom_call_target="tpu_custom_call" | custom-call | tf_op jit(solution)/shard_map/outer_step/pallas_call | solution.py:327
  53.9 0.0 copy-start
  53.9 1.6 %copy.8 = bf16[16,4096]{1,0:T(8,128)(2,1)} copy(bf16[16,4096]{1,0:T(8,128)(2,1)} %get-tuple-element.8) | data formatting | bytes 262144
  55.5 0.0 copy-done
  55.5 0.7 %copy.9 = f32[1,16,4096]{2,1,0:T(8,128)} copy(f32[1,16,4096]{2,1,0:T(8,128)S(1)} %bitcast.6) | data formatting | bytes 524288
Async XLA Ops:
  53.9 1.6 %copy-start = (f32[16,4096]{1,0:T(8,128)S(1)}, f32[16,4096]{1,0:T(8,128)}, u32[]{:S(2)}) copy-start(f32[16,4096]{1,0:T(8,128)} %get-tuple-element.5) | copy-start | bytes 786436

commit v4 on v3

--- a/solution.py
+++ b/solution.py
@@ -11,9 +11,10 @@
 MESH = pl.DeviceIdType.MESH
 decay_rate = 0.999
 f32, bf16 = jnp.float32, jnp.bfloat16
-WIDTHS = (256, 256, 256, 256)
+WIDTHS = (256, 384, 384)
 STARTS = tuple(sum(WIDTHS[:c]) for c in range(len(WIDTHS)))
 CHUNKS = range(len(WIDTHS))
+ORDER = "P0 U2 P1 A0 P2 S3 A1 S4 A2 X M0 M1 UP M2"
 
 
 def halves(value):
@@ -166,10 +167,6 @@
         def _():
             send(u1.at[j], u1r.at[yc], u1_s, u1_r, yc_peer(d))
 
-    pl.semaphore_wait(relay.at[0], 5)
-    for d in (1, 2, 3):
-        signal(relay.at[1], x_peer(d))
-
     local[5].wait()
     wait_bytes(a_in.at[0:384], xr.at[0])
     act_t = a_in[...].astype(f32).T.astype(bf16)
@@ -203,15 +200,20 @@
             at, who = pl.ds(across * 4 + 2 * side, 2), (r, hh * 4 + x)
             send(sc.at[c, at], sch.at[c, side], sch_s.at[c, side], sch_r.at[c, side], who)
             send(q[c].at[at], qh[c].at[side], qh_s.at[c, side], qh_r.at[c, side], who)
-
-    def send_plain(c):
+        if c == 0:
+            pl.semaphore_wait(relay.at[0], 5)
+            for d in (1, 2, 3):
+                signal(relay.at[1], x_peer(d))
         for xx in (2, 3):
             send_block(c, up, xx, x)
             send_block(c, down, xx - 2, 4 + x)
-        for d in (2, 1, 3):
-            send_block(c, h, (x + d) % 4, 8 + x)
         qr[c][pl.ds(8 + x, 1)] = q[c][pl.ds(f, 1)]
         scr[c, pl.ds(8 + x, 1)] = sc[c, pl.ds(f, 1)]
+
+    def send_beside():
+        for c in CHUNKS:
+            for d in (2, 1, 3):
+                send_block(c, h, (x + d) % 4, 8 + x)
 
     def send_sums(c):
         for side, hh in ((0, up), (1, down)):
@@ -222,42 +224,31 @@
             for xx in (0, 1):
                 send_block(c, hh, xx + 2 * side, 4 * side + x)
 
-    products(0)
-    pl.semaphore_wait(relay.at[1], 3)
-    send_plain(0)
-
-    u1r[pl.ds(yc, 1)] = u1[pl.ds(yc, 1)]
-    wait_bytes(u1r.at[0:7], u1_r)
-    u2[...] = functools.reduce(jnp.add, [u1r[i] for i in range(8)]).reshape(16, 8, 128)
-
-    @pl.loop(1, 16)
-    def _(d):
-        who = fsdp_peer(d)
-        send(u2.at[who[1]], u2r.at[f], u2_s, u2_r, who)
-
-    u2r[pl.ds(f, 1)] = u2[pl.ds(f, 1)]
-
-    products(1)
-    send_plain(1)
-    products(2)
-    send_plain(2)
-    send_sums(0)
-    products(3)
-    send_plain(3)
-    send_sums(1)
-    send_sums(2)
-
-    wait_bytes(u2r.at[0:15], u2_r)
-    s3[pl.ds(zl, 1)] = functools.reduce(jnp.add, [u2r[i] for i in range(16)])[None]
-    for d in (2, 1, 3):
-        send(s3.at[zl], s3.at[zl], s3_s, s3_r, z_peer(d))
-    send_sums(3)
-    wait_bytes(s3.at[0:3], s3_r)
-    s4[pl.ds(yc, 1)] = functools.reduce(jnp.add, [s3[i] for i in range(4)])[None]
-
-    @pl.loop(1, 8)
-    def _(d):
-        send(s4.at[yc], s4.at[yc], s4_s, s4_r, yc_peer(d))
+    def sum_fsdp():
+        pl.semaphore_wait(relay.at[1], 3)
+        u1r[pl.ds(yc, 1)] = u1[pl.ds(yc, 1)]
+        wait_bytes(u1r.at[0:7], u1_r)
+        u2[...] = functools.reduce(jnp.add, [u1r[i] for i in range(8)]).reshape(16, 8, 128)
+
+        @pl.loop(1, 16)
+        def _(d):
+            who = fsdp_peer(d)
+            send(u2.at[who[1]], u2r.at[f], u2_s, u2_r, who)
+
+        u2r[pl.ds(f, 1)] = u2[pl.ds(f, 1)]
+
+    def sum_z():
+        wait_bytes(u2r.at[0:15], u2_r)
+        s3[pl.ds(zl, 1)] = functools.reduce(jnp.add, [u2r[i] for i in range(16)])[None]
+        for d in (2, 1, 3):
+            send(s3.at[zl], s3.at[zl], s3_s, s3_r, z_peer(d))
+    def gather_yc():
+        wait_bytes(s3.at[0:3], s3_r)
+        s4[pl.ds(yc, 1)] = functools.reduce(jnp.add, [s3[i] for i in range(4)])[None]
+
+        @pl.loop(1, 8)
+        def _(d):
+            send(s4.at[yc], s4.at[yc], s4_s, s4_r, yc_peer(d))
 
     def new_momentum(c):
         width, groups = WIDTHS[c], WIDTHS[c] // 128
@@ -281,27 +272,29 @@
         for xx in range(4):
             start = 1024 * xx + STARTS[c]
             mo_v[:, start:start + width] = left_over[:, xx * width:(xx + 1) * width]
-
-    for c in CHUNKS[:-1]:
-        new_momentum(c)
-
-    wait_bytes(s4.at[0:7], s4_r)
-    total = s4[...]
-    power = jnp.sum(total * total, axis=1, keepdims=True)
-    scaled = (total / jnp.sqrt(power * (1.0 / 64.0) + 1e-06)).reshape(64, 128)
-    bands = []
-    for p in range(2):
-        spread = ((iota((128, 512), 1) >> 3) + 64 * p == iota((128, 512), 0)).astype(bf16)
-        wide = two_part(scaled, spread).reshape(8, 8, 512) * cv512[None]
-        bands.append(jnp.tanh(mix_rows(decode_rows, wide)))
-    for j in range(8):
-        upd_v[:, 512 * j:512 * (j + 1)] = jnp.concatenate([band[j] for band in bands], axis=0).astype(bf16)
-    out0 = pltpu.make_async_copy(upd_v, upd, out_sem.at[0])
-    out0.start()
-
-    new_momentum(CHUNKS[-1])
-    out1 = pltpu.make_async_copy(mo_v, mo, out_sem.at[1])
-    out1.start()
+            strip = pl.ds(start, width)
+            pltpu.make_async_copy(mo_v.at[:, strip], mo.at[:, strip], out_sem.at[1]).start()
+
+    def update():
+        wait_bytes(s4.at[0:7], s4_r)
+        total = s4[...]
+        power = jnp.sum(total * total, axis=1, keepdims=True)
+        scaled = (total / jnp.sqrt(power * (1.0 / 64.0) + 1e-06)).reshape(64, 128)
+        bands = []
+        for p in range(2):
+            spread = ((iota((128, 512), 1) >> 3) + 64 * p == iota((128, 512), 0)).astype(bf16)
+            wide = two_part(scaled, spread).reshape(8, 8, 512) * cv512[None]
+            bands.append(jnp.tanh(mix_rows(decode_rows, wide)))
+        for j in range(8):
+            upd_v[:, 512 * j:512 * (j + 1)] = jnp.concatenate([band[j] for band in bands], axis=0).astype(bf16)
+        pltpu.make_async_copy(upd_v, upd, out_sem.at[0]).start()
+
+    steps = {"U2": sum_fsdp, "S3": sum_z, "S4": gather_yc, "UP": update, "X": send_beside}
+    steps |= {f"P{c}": functools.partial(products, c) for c in CHUNKS}
+    steps |= {f"A{c}": functools.partial(send_sums, c) for c in CHUNKS}
+    steps |= {f"M{c}": functools.partial(new_momentum, c) for c in CHUNKS}
+    for step in ORDER.split():
+        steps[step]()
 
     wait_bytes(a_in.at[0:384], xs.at[0])
     for c in CHUNKS:
@@ -315,8 +308,21 @@
     wait_bytes(u2.at[0:15], u2_s)
     wait_bytes(s3.at[0:3], s3_s)
     wait_bytes(s4.at[0:7], s4_s)
-    out0.wait()
-    out1.wait()
+    wait_bytes(upd_v, out_sem.at[0])
+    wait_bytes(mo_v, out_sem.at[1])
+
+
+def hand_over(upd, mo, upd_out, mo_out, upd_v, mo_v, sem):
+    pairs = ((mo, mo_v, mo_out), (upd, upd_v, upd_out))
+    into = [pltpu.make_async_copy(src, held, sem.at[i]) for i, (src, held, _) in enumerate(pairs)]
+    out = [pltpu.make_async_copy(held, dst, sem.at[2 + i]) for i, (_, held, dst) in enumerate(pairs)]
+    for copy in into:
+        copy.start()
+    for before, after in zip(into, out):
+        before.wait()
+        after.start()
+    for copy in out:
+        copy.wait()
 
 
 def on_device(activations, cotangent, momentum, kept_index):
@@ -324,10 +330,11 @@
     dma = pltpu.SemaphoreType.DMA
     vmem = pltpu.VMEM
     n = len(WIDTHS)
+    out_shape = (jax.ShapeDtypeStruct((16, 4096), bf16), jax.ShapeDtypeStruct((16, 4096), f32))
     update, momentum_out = pl.pallas_call(
         kernel,
         name="outer_step",
-        out_shape=(jax.ShapeDtypeStruct((16, 4096), bf16), jax.ShapeDtypeStruct((16, 4096), f32)),
+        out_shape=out_shape,
         in_specs=[hbm] * 4,
         out_specs=(hbm, hbm),
         scratch_shapes=[
@@ -371,6 +378,15 @@
             collective_id=1, has_side_effects=True, vmem_limit_bytes=60 * 1024 * 1024
         ),
     )(kept_index, activations[0], cotangent[0], momentum[0])
+    update, momentum_out = pl.pallas_call(
+        hand_over,
+        name="hand_over",
+        out_shape=out_shape,
+        in_specs=[hbm] * 2,
+        out_specs=(hbm, hbm),
+        scratch_shapes=[vmem((16, 4096), bf16), vmem((16, 4096), f32), dma((4,))],
+        compiler_params=pltpu.CompilerParams(vmem_limit_bytes=60 * 1024 * 1024),
+    )(update, momentum_out)
     return update, momentum_out[None]
 
 

time: 56.4 us -> 52.6 us (0.933)
  the two profiles are of different devices: /device:TPU:3 before, /device:TPU:1 now
where the time goes in v4:
time: 52.6 us; the launch traced here: 52.5 us
  Pallas kernels  51.8 us (98%)
  between operations  0.64 us (1%)
    pallas_call x1, Pallas kernels, on_device(): pl.pallas_call(kernel, name='outer_step', out_shape=out_shape, in_specs=[...  50.1 us
    pallas_call x1, Pallas kernels, on_device(): pl.pallas_call(hand_over, name='hand_over', out_shape=out_shape, in_specs...  1.73 us

profile of v4, /device:TPU:1, one launch (start us, length us, event | category | flops | bytes accessed | tf_op | source)
XLA Modules:
  0.0 52.5 jit_solution(6955054319846753644)
XLA Ops:
  0.6 50.1 %outer_step.1 = (bf16[16,4096]{1,0:T(8,128)(2,1)}, f32[16,4096]{1,0:T(8,128)}) custom-call(s32[8]{0:T(128)} %kept_hbm.1, bf16[128,256]{1,0:T(8,128)(2,1)} %bitcast.6, bf16[128,4096]{1,0:T(8,128)(2,1)} %bitcast.4, f32[16,4096]{1,0:T(8,128)} %bitcast.5), custom_call_target="tpu_custom_call" | custom-call | tf_op jit(solution)/shard_map/outer_step/pallas_call | solution.py:334
  50.8 1.7 %hand_over.1 = (bf16[16,4096]{1,0:T(8,128)(2,1)}, f32[16,4096]{1,0:T(8,128)}) custom-call(bf16[16,4096]{1,0:T(8,128)(2,1)} %get-tuple-element.6.upd, f32[16,4096]{1,0:T(8,128)} %get-tuple-element.7.mo), custom_call_target="tpu_custom_call" | custom-call | tf_op jit(solution)/shard_map/hand_over/pallas_call | solution.py:381

commit v5 on v4

--- a/solution.py
+++ b/solution.py
@@ -11,10 +11,10 @@
 MESH = pl.DeviceIdType.MESH
 decay_rate = 0.999
 f32, bf16 = jnp.float32, jnp.bfloat16
-WIDTHS = (256, 384, 384)
+WIDTHS = (128, 384, 512)
 STARTS = tuple(sum(WIDTHS[:c]) for c in range(len(WIDTHS)))
 CHUNKS = range(len(WIDTHS))
-ORDER = "P0 U2 P1 A0 P2 S3 A1 S4 A2 X M0 M1 UP M2"
+ORDER = ('P0', 'U2', 'P1', 'A0', 'P2', 'S3', 'A1', 'S4', 'A2', 'X', 'M0', 'M1', 'UP', 'M2')
 
 
 def halves(value):
@@ -167,6 +167,10 @@
         def _():
             send(u1.at[j], u1r.at[yc], u1_s, u1_r, yc_peer(d))
 
+    pl.semaphore_wait(relay.at[0], 5)
+    for d in (1, 2, 3):
+        signal(relay.at[1], x_peer(d))
+
     local[5].wait()
     wait_bytes(a_in.at[0:384], xr.at[0])
     act_t = a_in[...].astype(f32).T.astype(bf16)
@@ -200,10 +204,6 @@
             at, who = pl.ds(across * 4 + 2 * side, 2), (r, hh * 4 + x)
             send(sc.at[c, at], sch.at[c, side], sch_s.at[c, side], sch_r.at[c, side], who)
             send(q[c].at[at], qh[c].at[side], qh_s.at[c, side], qh_r.at[c, side], who)
-        if c == 0:
-            pl.semaphore_wait(relay.at[0], 5)
-            for d in (1, 2, 3):
-                signal(relay.at[1], x_peer(d))
         for xx in (2, 3):
             send_block(c, up, xx, x)
             send_block(c, down, xx - 2, 4 + x)
@@ -293,7 +293,7 @@
     steps |= {f"P{c}": functools.partial(products, c) for c in CHUNKS}
     steps |= {f"A{c}": functools.partial(send_sums, c) for c in CHUNKS}
     steps |= {f"M{c}": functools.partial(new_momentum, c) for c in CHUNKS}
-    for step in ORDER.split():
+    for step in ORDER:
         steps[step]()
 
     wait_bytes(a_in.at[0:384], xs.at[0])

time: 52.6 us -> 52.4 us (level)
  Pallas kernels: 51.8 us -> 51.1 us
    pallas_call x1, Pallas kernels: 50.1 us -> 49.4 us  [on_device(): pl.pallas_call(kernel, name='outer_step', out_shape=out_shape, in_specs=[...]
where the time goes in v5:
time: 52.4 us; the launch traced here: 51.8 us
  Pallas kernels  51.1 us (98%)
  between operations  0.64 us (1%)
    pallas_call x1, Pallas kernels, on_device(): pl.pallas_call(kernel, name='outer_step', out_shape=out_shape, in_specs=[...  49.4 us
    pallas_call x1, Pallas kernels, on_device(): pl.pallas_call(hand_over, name='hand_over', out_shape=out_shape, in_specs...  1.73 us

profile of v5, /device:TPU:1, one launch (start us, length us, event | category | flops | bytes accessed | tf_op | source)
XLA Modules:
  0.0 51.8 jit_solution(14043719198594865113)
XLA Ops:
  0.6 49.4 %outer_step.1 = (bf16[16,4096]{1,0:T(8,128)(2,1)}, f32[16,4096]{1,0:T(8,128)}) custom-call(s32[8]{0:T(128)} %kept_hbm.1, bf16[128,256]{1,0:T(8,128)(2,1)} %bitcast.6, bf16[128,4096]{1,0:T(8,128)(2,1)} %bitcast.4, f32[16,4096]{1,0:T(8,128)} %bitcast.5), custom_call_target="tpu_custom_call" | custom-call | tf_op jit(solution)/shard_map/outer_step/pallas_call | solution.py:334
  50.0 1.7 %hand_over.1 = (bf16[16,4096]{1,0:T(8,128)(2,1)}, f32[16,4096]{1,0:T(8,128)}) custom-call(bf16[16,4096]{1,0:T(8,128)(2,1)} %get-tuple-element.6.upd, f32[16,4096]{1,0:T(8,128)} %get-tuple-element.7.mo), custom_call_target="tpu_custom_call" | custom-call | tf_op jit(solution)/shard_map/hand_over/pallas_call | solution.py:381

commit v6 on v5

--- a/solution.py
+++ b/solution.py
@@ -167,14 +167,13 @@
         def _():
             send(u1.at[j], u1r.at[yc], u1_s, u1_r, yc_peer(d))
 
-    pl.semaphore_wait(relay.at[0], 5)
-    for d in (1, 2, 3):
-        signal(relay.at[1], x_peer(d))
-
     local[5].wait()
     wait_bytes(a_in.at[0:384], xr.at[0])
     act_t = a_in[...].astype(f32).T.astype(bf16)
     local[6].wait()
+    pl.semaphore_wait(relay.at[0], 5)
+    for d in (1, 2, 3):
+        signal(relay.at[1], x_peer(d))
 
     up, down, across = (h + 1) % 4, (h + 3) % 4, (h + 2) % 4
 
@@ -199,14 +198,22 @@
         wait_bytes(c_in.at[0:384, pl.ds(STARTS[c], WIDTHS[c])], xr.at[1 + c])
         grad = dot(act_t, c_in[:, STARTS[c]:STARTS[c] + WIDTHS[c]]).reshape(16, 16, WIDTHS[c])
         g[c][...] = grad
-        quantize(c, slice(None), grad)
+
+        def ready(first, count):
+            at = pl.ds(first, count)
+            quantize(c, at, g[c][at])
+
+        ready(across * 4, 4)
         for side, hh in ((0, up), (1, down)):
             at, who = pl.ds(across * 4 + 2 * side, 2), (r, hh * 4 + x)
             send(sc.at[c, at], sch.at[c, side], sch_s.at[c, side], sch_r.at[c, side], who)
             send(q[c].at[at], qh[c].at[side], qh_s.at[c, side], qh_r.at[c, side], who)
+        ready(up * 4 + 2, 2)
+        ready(down * 4, 2)
         for xx in (2, 3):
             send_block(c, up, xx, x)
             send_block(c, down, xx - 2, 4 + x)
+        ready(h * 4, 4)
         qr[c][pl.ds(8 + x, 1)] = q[c][pl.ds(f, 1)]
         scr[c, pl.ds(8 + x, 1)] = sc[c, pl.ds(f, 1)]
 

time: 52.4 us -> 52.4 us (level)
  no operation moved by 1% of the time
where the time goes in v6:
time: 52.4 us; the launch traced here: 51.8 us
  Pallas kernels  51.1 us (98%)
  between operations  0.64 us (1%)
    pallas_call x1, Pallas kernels, on_device(): pl.pallas_call(kernel, name='outer_step', out_shape=out_shape, in_specs=[...  49.4 us
    pallas_call x1, Pallas kernels, on_device(): pl.pallas_call(hand_over, name='hand_over', out_shape=out_shape, in_specs...  1.73 us

profile of v6, /device:TPU:1, one launch (start us, length us, event | category | flops | bytes accessed | tf_op | source)
XLA Modules:
  0.0 51.8 jit_solution(12461632171063972827)
XLA Ops:
  0.6 49.4 %outer_step.1 = (bf16[16,4096]{1,0:T(8,128)(2,1)}, f32[16,4096]{1,0:T(8,128)}) custom-call(s32[8]{0:T(128)} %kept_hbm.1, bf16[128,256]{1,0:T(8,128)(2,1)} %bitcast.6, bf16[128,4096]{1,0:T(8,128)(2,1)} %bitcast.4, f32[16,4096]{1,0:T(8,128)} %bitcast.5), custom_call_target="tpu_custom_call" | custom-call | tf_op jit(solution)/shard_map/outer_step/pallas_call | solution.py:341
  50.0 1.7 %hand_over.1 = (bf16[16,4096]{1,0:T(8,128)(2,1)}, f32[16,4096]{1,0:T(8,128)}) custom-call(bf16[16,4096]{1,0:T(8,128)(2,1)} %get-tuple-element.6.upd, f32[16,4096]{1,0:T(8,128)} %get-tuple-element.7.mo), custom_call_target="tpu_custom_call" | custom-call | tf_op jit(solution)/shard_map/hand_over/pallas_call | solution.py:388

commit v7 on v5

--- a/solution.py
+++ b/solution.py
@@ -151,21 +151,25 @@
     for at in (2, 3, 4):
         local[at].wait()
 
-    @pl.loop(1, 9)
-    def _(d):
-        j = (yc + d) % 8
+    def folded(j):
         columns = pl.ds(pl.multiple_of(j * 512, 512), 512)
         mix = dot(mixed_act, c_own[:, columns])
         rows = mix_rows(encode_rows, (m_in[:, columns] * decay_rate).reshape(2, 8, 512))
         mix = (jnp.concatenate([mix.reshape(32, 8, 512), rows], axis=0) * cv512[None]).reshape(272, 512)
-        sums = two_part(mix, gather)
-        u1[j] = sums[:128] + pltpu.roll(sums[128:256], 64, 1)
+        return two_part(mix, gather)
+
+    @pl.loop(0, 4)
+    def _(i):
+        pair = [(yc + 2 * i + 1) % 8, (yc + 2 * i + 2) % 8]
         at = pl.ds(pl.multiple_of(f * 8, 8), 8)
-        u1[j, at, :] = u1[j, at, :] + sums[256:264] + pltpu.roll(sums[264:272], 64, 1)
-
-        @pl.when(d < 8)
+        for j, sums in zip(pair, [folded(j) for j in pair]):
+            u1[j] = sums[:128] + pltpu.roll(sums[128:256], 64, 1)
+            u1[j, at, :] = u1[j, at, :] + sums[256:264] + pltpu.roll(sums[264:272], 64, 1)
+        send(u1.at[pair[0]], u1r.at[yc], u1_s, u1_r, yc_peer(2 * i + 1))
+
+        @pl.when(i < 3)
         def _():
-            send(u1.at[j], u1r.at[yc], u1_s, u1_r, yc_peer(d))
+            send(u1.at[pair[1]], u1r.at[yc], u1_s, u1_r, yc_peer(2 * i + 2))
 
     pl.semaphore_wait(relay.at[0], 5)
     for d in (1, 2, 3):

time: 52.4 us -> 52.4 us (level)
  no operation moved by 1% of the time
where the time goes in v7:
time: 52.4 us; the launch traced here: 51.5 us
  Pallas kernels  50.8 us (97%)
  between operations  0.64 us (1%)
    pallas_call x1, Pallas kernels, on_device(): pl.pallas_call(kernel, name='outer_step', out_shape=out_shape, in_specs=[...  49.1 us
    pallas_call x1, Pallas kernels, on_device(): pl.pallas_call(hand_over, name='hand_over', out_shape=out_shape, in_specs...  1.73 us

profile of v7, /device:TPU:1, one launch (start us, length us, event | category | flops | bytes accessed | tf_op | source)
XLA Modules:
  0.0 51.5 jit_solution(439595227863406240)
XLA Ops:
  0.6 49.1 %outer_step.1 = (bf16[16,4096]{1,0:T(8,128)(2,1)}, f32[16,4096]{1,0:T(8,128)}) custom-call(s32[8]{0:T(128)} %kept_hbm.1, bf16[128,256]{1,0:T(8,128)(2,1)} %bitcast.6, bf16[128,4096]{1,0:T(8,128)(2,1)} %bitcast.4, f32[16,4096]{1,0:T(8,128)} %bitcast.5), custom_call_target="tpu_custom_call" | custom-call | tf_op jit(solution)/shard_map/outer_step/pallas_call | solution.py:338
  49.7 1.7 %hand_over.1 = (bf16[16,4096]{1,0:T(8,128)(2,1)}, f32[16,4096]{1,0:T(8,128)}) custom-call(bf16[16,4096]{1,0:T(8,128)(2,1)} %get-tuple-element.6.upd, f32[16,4096]{1,0:T(8,128)} %get-tuple-element.7.mo), custom_call_target="tpu_custom_call" | custom-call | tf_op jit(solution)/shard_map/hand_over/pallas_call | solution.py:385

commit v8 on v7

--- a/solution.py
+++ b/solution.py
@@ -171,14 +171,13 @@
         def _():
             send(u1.at[pair[1]], u1r.at[yc], u1_s, u1_r, yc_peer(2 * i + 2))
 
-    pl.semaphore_wait(relay.at[0], 5)
-    for d in (1, 2, 3):
-        signal(relay.at[1], x_peer(d))
-
     local[5].wait()
     wait_bytes(a_in.at[0:384], xr.at[0])
     act_t = a_in[...].astype(f32).T.astype(bf16)
     local[6].wait()
+    pl.semaphore_wait(relay.at[0], 5)
+    for d in (1, 2, 3):
+        signal(relay.at[1], x_peer(d))
 
     up, down, across = (h + 1) % 4, (h + 3) % 4, (h + 2) % 4
 
@@ -203,14 +202,22 @@
         wait_bytes(c_in.at[0:384, pl.ds(STARTS[c], WIDTHS[c])], xr.at[1 + c])
         grad = dot(act_t, c_in[:, STARTS[c]:STARTS[c] + WIDTHS[c]]).reshape(16, 16, WIDTHS[c])
         g[c][...] = grad
-        quantize(c, slice(None), grad)
+
+        def ready(first, count):
+            at = pl.ds(first, count)
+            quantize(c, at, g[c][at])
+
+        ready(across * 4, 4)
         for side, hh in ((0, up), (1, down)):
             at, who = pl.ds(across * 4 + 2 * side, 2), (r, hh * 4 + x)
             send(sc.at[c, at], sch.at[c, side], sch_s.at[c, side], sch_r.at[c, side], who)
             send(q[c].at[at], qh[c].at[side], qh_s.at[c, side], qh_r.at[c, side], who)
+        ready(up * 4 + 2, 2)
+        ready(down * 4, 2)
         for xx in (2, 3):
             send_block(c, up, xx, x)
             send_block(c, down, xx - 2, 4 + x)
+        ready(h * 4, 4)
         qr[c][pl.ds(8 + x, 1)] = q[c][pl.ds(f, 1)]
         scr[c, pl.ds(8 + x, 1)] = sc[c, pl.ds(f, 1)]
 

time: 52.4 us -> 52.4 us (level)
  no operation moved by 1% of the time
where the time goes in v8:
time: 52.4 us; the launch traced here: 51.6 us
  Pallas kernels  51 us (97%)
  between operations  0.64 us (1%)
    pallas_call x1, Pallas kernels, on_device(): pl.pallas_call(kernel, name='outer_step', out_shape=out_shape, in_specs=[...  49.2 us
    pallas_call x1, Pallas kernels, on_device(): pl.pallas_call(hand_over, name='hand_over', out_shape=out_shape, in_specs...  1.73 us

profile of v8, /device:TPU:1, one launch (start us, length us, event | category | flops | bytes accessed | tf_op | source)
XLA Modules:
  0.0 51.6 jit_solution(17012626282316552030)
XLA Ops:
  0.6 49.2 %outer_step.1 = (bf16[16,4096]{1,0:T(8,128)(2,1)}, f32[16,4096]{1,0:T(8,128)}) custom-call(s32[8]{0:T(128)} %kept_hbm.1, bf16[128,256]{1,0:T(8,128)(2,1)} %bitcast.6, bf16[128,4096]{1,0:T(8,128)(2,1)} %bitcast.4, f32[16,4096]{1,0:T(8,128)} %bitcast.5), custom_call_target="tpu_custom_call" | custom-call | tf_op jit(solution)/shard_map/outer_step/pallas_call | solution.py:345
  49.9 1.7 %hand_over.1 = (bf16[16,4096]{1,0:T(8,128)(2,1)}, f32[16,4096]{1,0:T(8,128)}) custom-call(bf16[16,4096]{1,0:T(8,128)(2,1)} %get-tuple-element.6.upd, f32[16,4096]{1,0:T(8,128)} %get-tuple-element.7.mo), custom_call_target="tpu_custom_call" | custom-call | tf_op jit(solution)/shard_map/hand_over/pallas_call | solution.py:392
